TPU v7x, 32 devices: a whole 2x2x4 slice. The times are simulated.
32 devices in a mesh: parts: 2 (over x), shard: 4 (over y, core), sub: 4 (over z).
Axes of the slice: x: 2, y: 2, z: 4, core: 2. Of those that a mesh axis runs over, the one named last changes fastest.
Arguments:
- host_factors: float32 [8192, 256], P(('parts', 'shard', 'sub')), parts along dimension 0, may hold values from -6 to 6
- token_ids: int32 [8192, 16], P(('parts', 'shard', 'sub')), parts along dimension 0, may hold values from 0 to 131071, as said below
- counts: int32 [8192, 16], P(('parts', 'shard', 'sub')), parts along dimension 0, may hold values from 1 to 63
- lengths: int32 [8192], P(('parts', 'shard', 'sub')), parts along dimension 0, may hold values from 2 to 16
- token_factors: bfloat16 [262144, 256], P(('parts', 'shard', 'sub')), parts along dimension 0, as said below
Outputs:
- new_factors: float32 [8192, 256], P(('parts', 'shard', 'sub')), parts along dimension 0
There are 2 independent parts, one for each index of `parts`. A program takes and returns all parts, laid end to end along the dimension named above; each array names one. Nothing has to cross between parts.
Inputs may be any that keep to these rules, and one draw needn't show every extreme that they name: `token_ids`: token id t belongs to the device t // 8192 along shard+sub. Among the live slots of one device's 256 hosts, at most 256 name tokens of any one owner, and in every draw some owner is named exactly 256 times by each device's live slots. `token_factors`: factors of order one over the square root of the token count.
All inputs are finite; a program needn't handle non-finite values.
Results may differ from a plain program's by a relative error of at most 0.0003.
Values may be sent and summed in bfloat16 or wider, within the bound.
A program may use at most 64 MiB of HBM per device.

v0:
```python
import math

import jax
import jax.numpy as jnp
from jax import lax
from jax.sharding import PartitionSpec as P

CG_STEPS = 3


CONFIDENCE_SCALE = 40.0
RIDGE_WEIGHT = 0.1
SMALL_EPSILON = 1e-06
HIGHEST = lax.Precision.HIGHEST


def system_product(gram_matrix, gathered, weights, vectors):
    projected = jnp.einsum(
        "hsr,hr->hs", gathered, vectors, precision=HIGHEST, preferred_element_type=jnp.float32
    )
    spread_back = jnp.einsum(
        "hsr,hs->hr",
        gathered,
        weights * projected,
        precision=HIGHEST,
        preferred_element_type=jnp.float32,
    )
    return jnp.dot(vectors, gram_matrix, precision=HIGHEST) + RIDGE_WEIGHT * vectors + spread_back


def owner_ranks(owner_hot, block_rows):
    total_rows, owner_width = owner_hot.shape
    block_count = total_rows // block_rows
    blocked = owner_hot.reshape(block_count, block_rows, owner_width)
    position = jnp.arange(block_rows, dtype=jnp.int32)
    lower_mask = (position[:, None] > position[None, :]).astype(jnp.bfloat16)
    within = jnp.einsum("ij,bjk->bik", lower_mask, blocked, preferred_element_type=jnp.float32)
    totals = jnp.sum(blocked.astype(jnp.float32), axis=1)
    block_index = jnp.arange(block_count, dtype=jnp.int32)
    block_lower = (block_index[:, None] > block_index[None, :]).astype(jnp.float32)
    before = jnp.dot(block_lower, totals, precision=HIGHEST)
    running = within + before[:, None, :]
    ranks = jnp.sum(running * blocked.astype(jnp.float32), axis=2)
    return ranks.reshape(total_rows).astype(jnp.int32)


def shards(host_factors, token_ids, counts, lengths, token_factors):
    device_count = lax.axis_size(("shard", "sub"))
    token_rows = token_factors.shape[0]
    host_count, slot_count = token_ids.shape
    factor_width = host_factors.shape[1]
    capacity = max(4, host_count * slot_count // device_count)
    partial_gram = lax.dot_general(
        token_factors, token_factors, (((0,), (0,)), ((), ())), preferred_element_type=jnp.float32
    )
    gram_matrix = lax.psum(partial_gram, ("shard", "sub"))
    alive_mask = jnp.arange(slot_count, dtype=jnp.int32)[None, :] < lengths[:, None]
    owners = jnp.where(alive_mask, token_ids // token_rows, device_count).reshape(-1)
    local_rows = (token_ids % token_rows).reshape(-1)
    total_rows = host_count * slot_count
    block_rows = math.gcd(total_rows, 512)
    block_count = total_rows // block_rows
    owner_hot = (owners[:, None] == jnp.arange(device_count + 1, dtype=jnp.int32)[None, :]).astype(
        jnp.bfloat16
    )
    ranks = owner_ranks(owner_hot, block_rows)
    buffer_slot = owners * capacity + ranks
    capacity_index = jnp.arange(capacity, dtype=jnp.int32)

    def place_block(total, packed):
        hot_block, row_block, rank_block = packed
        valued = (
            hot_block[:, :device_count].astype(jnp.float32) * row_block.astype(jnp.float32)[:, None]
        )
        rank_hot = (rank_block[:, None] == capacity_index[None, :]).astype(jnp.float32)
        placed = lax.dot_general(
            valued,
            rank_hot,
            (((0,), (0,)), ((), ())),
            precision=HIGHEST,
            preferred_element_type=jnp.float32,
        )
        return (total + placed, None)

    request_table, unused = lax.scan(
        place_block,
        jnp.zeros((device_count, capacity), jnp.float32),
        (
            owner_hot.reshape(block_count, block_rows, device_count + 1),
            local_rows.reshape(block_count, block_rows),
            ranks.reshape(block_count, block_rows),
        ),
    )
    requests = request_table.astype(jnp.int32)
    location = jnp.minimum(buffer_slot, device_count * capacity - 1)
    located_rows = token_factors[
        lax.all_to_all(requests, ("shard", "sub"), split_axis=0, concat_axis=0, tiled=True)
    ]
    fetched = lax.all_to_all(
        located_rows, ("shard", "sub"), split_axis=0, concat_axis=0, tiled=True
    )
    fetched = fetched.reshape(device_count * capacity, factor_width)
    gathered = fetched[location].reshape(host_count, slot_count, factor_width)
    scaled = CONFIDENCE_SCALE * counts.astype(jnp.float32)
    weights = jnp.where(alive_mask, scaled, jnp.zeros_like(scaled))
    targets = jnp.where(alive_mask, 1.0 + scaled, jnp.zeros_like(scaled))
    target_sum = jnp.einsum(
        "hsr,hs->hr", gathered, targets, precision=HIGHEST, preferred_element_type=jnp.float32
    )
    iterate = host_factors
    residual = target_sum - system_product(gram_matrix, gathered, weights, iterate)
    direction = residual
    norm_now = jnp.sum(residual * residual, axis=1, keepdims=True)
    for iteration in range(CG_STEPS):
        image = system_product(gram_matrix, gathered, weights, direction)
        step_size = norm_now / (jnp.sum(direction * image, axis=1, keepdims=True) + SMALL_EPSILON)
        iterate = iterate + step_size * direction
        residual = residual - step_size * image
        norm_next = jnp.sum(residual * residual, axis=1, keepdims=True)
        direction = residual + norm_next / (norm_now + SMALL_EPSILON) * direction
        norm_now = norm_next
    return iterate


def solution(mesh):
    placed = (
        P(("parts", "shard", "sub"), None),
        P(("parts", "shard", "sub"), None),
        P(("parts", "shard", "sub"), None),
        P(("parts", "shard", "sub")),
        P(("parts", "shard", "sub"), None),
    )
    return jax.shard_map(
        shards,
        mesh=mesh,
        in_specs=placed,
        out_specs=P(("parts", "shard", "sub"), None),
        check_vma=False,
    )
```

profile of v0, /device:TPU:0, one launch (start us, length us, event | category | flops | bytes accessed | tf_op | source)
XLA Modules:
  0.0 184.4 jit_solution(11979470280936332216)
XLA Ops:
  6.5 0.7 broadcast_multiply_fusion
  7.3 0.1 copy.17
  7.4 0.1 eq.34
  7.5 0.1 convert_reduce_fusion
  7.7 0.1 fusion.39
  7.8 0.3 fusion.24
  8.2 0.1 copy.18
  8.3 0.1 reshape_reshape.3
  8.4 3.0 %while.11 = (s32[]{:T(128)}, f32[16,256]{1,0:T(8,128)S(1)}, bf16[8,512,17]{1,2,0:T(8,128)(2,1)S(1)}, s32[8,512]{1,0:T(8,128)S(1)}, s32[8,512]{1,0:T(8,128)S(1)}, /*index=5*/s32[]{:T(128)}, s32[]{:T(128)}) while((s32[]{:T(128)}, f32[16,256]{1,0:T(8,128)S(1)}, bf16[8,512,17]{1,2,0:T(8,128)(2,1)S(1)}, s32[8,512]{1,0:T(8,128)S(1)}, ...), condition=%wide.region_3.4_spmd.clone, body=%wide.region_2.3_spmd.clone.sunk | while | flops 25321988 | bytes 96351 | solution.py:85
  8.4 0.3 convolution_add_fusion.6
  8.8 0.3 convolution_add_fusion.6
  9.2 0.3 convolution_add_fusion.6
  9.6 0.3 convolution_add_fusion.6
  10.0 0.3 convolution_add_fusion.6
  10.3 0.3 convolution_add_fusion.6
  10.7 0.3 convolution_add_fusion.6
  11.1 0.3 convolution_add_fusion.6
  11.5 13.6 %all_to_all.17 = s32[16,1,256]{2,1,0:T(1,128)S(1)} all-to-all(s32[16,1,256]{2,1,0:T(1,128)S(1)} %all_to_all.11), channel_id=1, replica_groups=mesh['parts'=2,'shard'=4,'sub'=4] {'shard','sub'}, dimensions={0} | all-to-all | bytes 32768 | tf_op jit(solution)/shard_map/all_to_all | solution.py:97
  25.1 18.6 %gather_fusion = bf16[4096,256]{1,0:T(8,128)(2,1)} fusion(bf16[8192,256]{1,0:T(8,128)(2,1)} %param.11, s32[4096]{0:T(1024)S(1)} %broadcast_clamp_fusion.1), kind=kCustom, calls=%fused_computation | custom fusion | bytes 4210688 | tf_op jit(solution)/shard_map/gather | solution.py:96
  43.7 3.7 %all-to-all-start.1 = ((bf16[16,256,256]{2,1,0:T(8,128)(2,1)}), bf16[16,256,256]{2,1,0:T(8,128)(2,1)S(1)}, u32[]{:S(2)}, u32[]{:S(2)}) async-start(bf16[16,256,256]{2,1,0:T(8,128)(2,1)} %bitcast.70), calls=%async_computation.1 | async-start | bytes 4194304 | tf_op jit(solution)/shard_map/all_to_all | solution.py:99
  47.5 5.5 %fusion.41 = f32[256,256]{1,0:T(8,128)} fusion(bf16[8192,256]{1,0:T(8,128)(2,1)} %param.11), kind=kOutput, calls=%fused_computation.93 | convolution fusion | flops 1073741824 | bytes 4456448 | tf_op jit(solution)/shard_map/dot_general | solution.py:53
  53.0 0.1 copy.19
  53.1 0.1 mul.130
  53.2 0.1 copy.21
  53.4 45.2 %all-to-all-done.1 = bf16[16,256,256]{2,1,0:T(8,128)(2,1)S(1)} async-done(((bf16[16,256,256]{2,1,0:T(8,128)(2,1)}), bf16[16,256,256]{2,1,0:T(8,128)(2,1)S(1)}, u32[]{:S(2)}, u32[]{:S(2)}) %all-to-all-start.1) | async-done | bytes 2097184 | tf_op jit(solution)/shard_map/all_to_all | solution.py:99
  98.7 16.9 %gather_fusion.1 = bf16[4096,256]{1,0:T(8,128)(2,1)} fusion(bf16[4096,256]{1,0:T(8,128)(2,1)S(1)} %bitcast.65, s32[4096]{0:T(1024)S(1)} %broadcast_clamp_fusion), kind=kCustom, calls=%fused_computation.1 | custom fusion | bytes 4210688 | tf_op jit(solution)/shard_map/gather | solution.py:103
  115.6 3.5 %fusion.29 = f32[256,1,16]{2,1,0:T(1,128)S(1)} fusion(bf16[256,16,256]{2,1,0:T(8,128)(2,1)} %bitcast.66, f32[256,256,1]{1,0,2:T(8,128)S(1)} %bitcast.71), kind=kOutput, calls=%fused_computation.50 | convolution fusion | flops 12582912 | bytes 2375680 | tf_op jit(solution)/shard_map/hsr,hr->hs/dot_general | solution.py:18
  119.1 0.1 copy.28
  119.2 0.1 copy.60
  119.3 0.1 copy.61
  119.4 3.0 %fusion.11 = (f32[256,256]{1,0:T(8,128)S(1)}, f32[256,256]{1,0:T(8,128)S(1)}) fusion(f32[256,16]{1,0:T(8,128)S(1)} %copy.61, bf16[4096,256]{1,0:T(8,128)(2,1)S(1)} %copy-done, f32[256,16]{1,0:T(8,128)S(1)} %copy.60), kind=kLoop, calls=%fused_computation.25 | loop fusion | flops 5111808 | bytes 2654208
  122.4 0.1 copy.26
  122.5 0.8 copy.32
  123.4 36.0 %all-reduce.2.cloned.1.call-done = f32[256,256]{1,0:T(8,128)} async-done(((f32[256,256]{1,0:T(8,128)}), f32[256,256]{1,0:T(8,128)}) %all-reduce.2.cloned.1.call-update) | async-done | bytes 262160 | tf_op jit(solution)/shard_map/psum | solution.py:56
  159.4 1.7 fusion.23
  161.1 0.1 copy.69
  161.2 0.6 fusion.7
  161.9 0.1 copy.70
  162.0 1.5 fusion.12
  163.5 0.1 copy.41
  163.7 0.6 multiply_reduce_fusion.3
  164.3 0.1 multiply_reduce_fusion.2
  164.4 0.5 copy-done.10
  164.9 0.1 copy-done.6
  165.0 0.1 copy.76
  165.1 0.6 fusion.8
  165.8 0.7 fusion.37
  166.5 0.1 copy.77
  166.6 2.2 %fusion.13 = f32[256,256]{1,0:T(8,128)} fusion(f32[256,16]{1,0:T(8,128)S(1)} %copy.77, bf16[4096,256]{1,0:T(8,128)(2,1)S(1)} %copy-done), kind=kLoop, calls=%fused_computation.27 | loop fusion | flops 3080192 | bytes 2375680
  168.8 1.1 copy.50
  169.9 0.6 multiply_reduce_fusion.1
  170.5 0.1 multiply_reduce_fusion
  170.7 0.4 copy-done.8
  171.1 0.1 copy-done.9
  171.2 0.1 copy.82
  171.3 0.6 fusion.9
  172.0 0.7 fusion.36
  172.7 0.1 copy.83
  172.8 1.5 fusion.14
  174.3 0.1 copy.59
  174.4 0.6 fusion.25
  175.0 0.7 add_divide_fusion
  175.7 1.0 multiply_add_fusion
  176.8 0.8 copy.22
  (57 shorter events, 1.1 us)
Async XLA Ops:
  43.7 55.0 %all-to-all-start.1 = ((bf16[16,256,256]{2,1,0:T(8,128)(2,1)}), bf16[16,256,256]{2,1,0:T(8,128)(2,1)S(1)}, u32[]{:S(2)}, u32[]{:S(2)}) async-start(bf16[16,256,256]{2,1,0:T(8,128)(2,1)} %bitcast.70), calls=%async_computation.1 | async-start | bytes 4194304 | tf_op jit(solution)/shard_map/all_to_all | solution.py:99
  47.4 5.8 %copy-start.3 = (f32[256,256]{1,0:T(8,128)S(1)}, f32[256,256]{1,0:T(8,128)}, u32[]{:S(2)}) copy-start(f32[256,256]{1,0:T(8,128)} %param.7) | copy-start | bytes 786436
  47.4 111.9 %all-reduce.2.cloned.1.call-start = ((), (), s32[]{:S(2)}) async-start(), calls=%async_computation.2 | async-start | bytes 524288 | tf_op jit(solution)/shard_map/psum | solution.py:56
  53.4 106.0 %copy-start.2 = (f32[256,256]{0,1:T(8,128)}, f32[256,256]{0,1:T(8,128)S(1)}, u32[]{:S(2)}) copy-start(f32[256,256]{0,1:T(8,128)S(1)} %copy.21) | copy-start | bytes 786436
  98.7 20.5 %copy-start.4 = (s32[256,16]{0,1:T(8,128)S(1)}, s32[256,16]{0,1:T(8,128)}, u32[]{:S(2)}) copy-start(s32[256,16]{0,1:T(8,128)} %param.9) | copy-start | bytes 49156
  98.7 20.5 %copy-start.5 = (s32[256]{0:T(256)S(1)}, s32[256]{0:T(256)}, u32[]{:S(2)}) copy-start(s32[256]{0:T(256)} %param.10) | copy-start | bytes 3076
  115.6 3.8 %copy-start = (bf16[4096,256]{1,0:T(8,128)(2,1)S(1)}, bf16[4096,256]{1,0:T(8,128)(2,1)}, u32[]{:S(2)}) copy-start(bf16[4096,256]{1,0:T(8,128)(2,1)} %gather_fusion.1) | copy-start | bytes 6291460
  159.4 4.3 %copy-start.1 = (f32[256,256]{1,0:T(8,128)S(1)}, f32[256,256]{1,0:T(8,128)}, u32[]{:S(2)}) copy-start(f32[256,256]{1,0:T(8,128)} %all-reduce.2.cloned.1.call-done) | copy-start | bytes 786436
  164.3 0.6 copy-start.10
  164.4 0.6 copy-start.6
  165.8 4.7 %copy-start.7 = (f32[256]{0:T(256)S(1)}, f32[256]{0:T(256)}, u32[]{:S(2)}) copy-start(f32[256]{0:T(256)} %copy-done.6) | copy-start | bytes 3076
  170.5 0.6 copy-start.8
  170.6 0.6 copy-start.9
Sparse Core Ops, SparseCore 0:
  53.1 106.2 all-reduce.1
where the time goes:
time: 185 us; the launch traced here: 184 us
  waiting for transfers between devices  81.3 us (44%)
  local copies, waits for them, and re-layouts  41.7 us (23%)
  matrix products  15.3 us (8%)
  other arithmetic  14.8 us (8%)
  between operations  13.8 us (7%)
  blocking collectives  13.6 us (7%)
  starting transfers between devices  3.76 us (2%)
    all_to_all x1, waiting for transfers between devices, shards(): lax.all_to_all(located_rows, ('shard', 'sub'), split_axis=0, concat_axis=...  45.2 us
    psum x1, waiting for transfers between devices, shards(): gram_matrix = lax.psum(partial_gram, ('shard', 'sub'))  36 us
    gather x1, local copies, waits for them, and re-layouts, shards(): token_factors[lax.all_to_all(requests, ('shard', 'sub'), split_axis=0, co...  18.6 us
    gather x1, local copies, waits for them, and re-layouts, shards(): gathered = fetched[location].reshape(host_count, slot_count, factor_width)  16.9 us
    all_to_all x1, blocking collectives, shards(): lax.all_to_all(requests, ('shard', 'sub'), split_axis=0, concat_axis=0, t...  13.6 us
    unnamed x9, other arithmetic  10 us
    dot_general x1, matrix products, shards(): lax.dot_general(token_factors, token_factors, (((0,), (0,)), ((), ())), p...  5.47 us
    all_to_all x1, starting transfers between devices, shards(): lax.all_to_all(located_rows, ('shard', 'sub'), split_axis=0, concat_axis=...  3.72 us
  transfers between devices with their start and end apart: 2, of which 2 were waited for; matrix products, arithmetic and copies ran while one was open for 17% of the time, Pallas kernels for 0%

commit v1 on v0

v1 whole, which is shorter than its diff:
```python
import functools
import math

import jax
import jax.numpy as jnp
from jax import lax
from jax.experimental import pallas as pl
from jax.experimental.pallas import tpu as pltpu
from jax.sharding import PartitionSpec as P

CG_STEPS = 3
CONFIDENCE_SCALE = 40.0
RIDGE_WEIGHT = 0.1
SMALL_EPSILON = 1e-06
HIGHEST = lax.Precision.HIGHEST
COUNT_SPAN = 64


def owner_ranks(owner_hot, block_rows):
    total_rows, owner_width = owner_hot.shape
    block_count = total_rows // block_rows
    blocked = owner_hot.reshape(block_count, block_rows, owner_width)
    position = jnp.arange(block_rows, dtype=jnp.int32)
    lower_mask = (position[:, None] > position[None, :]).astype(jnp.bfloat16)
    within = jnp.einsum("ij,bjk->bik", lower_mask, blocked, preferred_element_type=jnp.float32)
    totals = jnp.sum(blocked.astype(jnp.float32), axis=1)
    block_index = jnp.arange(block_count, dtype=jnp.int32)
    block_lower = (block_index[:, None] > block_index[None, :]).astype(jnp.float32)
    before = jnp.dot(block_lower, totals, precision=HIGHEST)
    running = within + before[:, None, :]
    ranks = jnp.sum(running * blocked.astype(jnp.float32), axis=2)
    return ranks.reshape(total_rows).astype(jnp.int32)


def request_tables(token_ids, counts, lengths, token_rows, device_count, capacity):
    host_count, slot_count = token_ids.shape
    alive_mask = jnp.arange(slot_count, dtype=jnp.int32)[None, :] < lengths[:, None]
    owners = jnp.where(alive_mask, token_ids // token_rows, device_count).reshape(-1)
    local_rows = (token_ids % token_rows).reshape(-1)
    hosts = jnp.arange(host_count, dtype=jnp.int32)[:, None]
    codes = ((hosts + 1) * COUNT_SPAN + counts).reshape(-1)
    total_rows = host_count * slot_count
    block_rows = math.gcd(total_rows, 512)
    block_count = total_rows // block_rows
    owner_hot = (owners[:, None] == jnp.arange(device_count + 1, dtype=jnp.int32)[None, :]).astype(
        jnp.bfloat16
    )
    ranks = owner_ranks(owner_hot, block_rows)
    capacity_index = jnp.arange(capacity, dtype=jnp.int32)

    def place_block(total, packed):
        hot_block, row_block, code_block, rank_block = packed
        hot = hot_block[:, :device_count].astype(jnp.float32)
        valued = jnp.concatenate(
            [
                hot * row_block.astype(jnp.float32)[:, None],
                hot * code_block.astype(jnp.float32)[:, None],
            ],
            axis=1,
        )
        rank_hot = (rank_block[:, None] == capacity_index[None, :]).astype(jnp.float32)
        placed = lax.dot_general(
            valued,
            rank_hot,
            (((0,), (0,)), ((), ())),
            precision=HIGHEST,
            preferred_element_type=jnp.float32,
        )
        return (total + placed, None)

    tables, unused = lax.scan(
        place_block,
        jnp.zeros((2 * device_count, capacity), jnp.float32),
        (
            owner_hot.reshape(block_count, block_rows, device_count + 1),
            local_rows.reshape(block_count, block_rows),
            codes.reshape(block_count, block_rows),
            ranks.reshape(block_count, block_rows),
        ),
    )
    return tables[:device_count], tables[device_count:].astype(jnp.int32)


def split_pair(values):
    high = values.astype(jnp.bfloat16)
    low = (values - high.astype(jnp.float32)).astype(jnp.bfloat16)
    return jnp.concatenate([high, low], axis=0)


def spread(capacity, rows_ref, code_ref, vectors, first, scratch_ref):
    host_count = vectors.shape[0]
    halves = split_pair(vectors)
    scratch_ref[...] = jnp.zeros_like(scratch_ref)
    row_host = lax.broadcasted_iota(jnp.int32, (host_count, capacity), 0) + 1

    @pl.loop(0, rows_ref.shape[0])
    def _(block):
        rows = rows_ref[block, :capacity, :]
        code = code_ref[pl.ds(block, 1), :]
        both = lax.dot_general(
            halves, rows, (((1,), (1,)), ((), ())), preferred_element_type=jnp.float32
        )
        inner = both[:host_count] + both[host_count:]
        weight = CONFIDENCE_SCALE * (code % COUNT_SPAN).astype(jnp.float32)
        if first:
            value = (1.0 + weight) - weight * inner
        else:
            value = weight * inner
        masked = jnp.where(row_host == code // COUNT_SPAN, value, 0.0)
        out = jnp.dot(split_pair(masked), rows, preferred_element_type=jnp.float32)
        scratch_ref[...] += out[:host_count] + out[host_count:]

    return scratch_ref[...]


def solve_body(capacity, rows_ref, code_ref, gram_ref, start_ref, out_ref, scratch_ref):
    def smooth(vectors):
        return (
            jnp.dot(
                vectors, gram_ref[...], precision=HIGHEST, preferred_element_type=jnp.float32
            )
            + RIDGE_WEIGHT * vectors
        )

    iterate = start_ref[...]
    residual = spread(capacity, rows_ref, code_ref, iterate, True, scratch_ref) - smooth(iterate)
    direction = residual
    norm_now = jnp.sum(residual * residual, axis=1, keepdims=True)
    for iteration in range(CG_STEPS):
        image = spread(capacity, rows_ref, code_ref, direction, False, scratch_ref) + smooth(
            direction
        )
        step_size = norm_now / (jnp.sum(direction * image, axis=1, keepdims=True) + SMALL_EPSILON)
        iterate = iterate + step_size * direction
        if iteration < CG_STEPS - 1:
            residual = residual - step_size * image
            norm_next = jnp.sum(residual * residual, axis=1, keepdims=True)
            direction = residual + norm_next / (norm_now + SMALL_EPSILON) * direction
            norm_now = norm_next
    out_ref[...] = iterate


def shards(host_factors, token_ids, counts, lengths, token_factors):
    axes = ("shard", "sub")
    device_count = lax.axis_size(axes)
    token_rows = token_factors.shape[0]
    host_count, slot_count = token_ids.shape
    width = host_factors.shape[1]
    capacity = max(4, host_count * slot_count // device_count)
    share = width // device_count
    partial_gram = lax.dot_general(
        token_factors, token_factors, (((0,), (0,)), ((), ())), preferred_element_type=jnp.float32
    )
    wanted, codes = request_tables(
        token_ids, counts, lengths, token_rows, device_count, capacity
    )
    outgoing = jnp.concatenate([partial_gram.reshape(device_count, share * width), wanted], axis=1)
    incoming = lax.all_to_all(outgoing, axes, split_axis=0, concat_axis=0, tiled=True)
    requests = incoming[:, share * width :].astype(jnp.int32)
    gram_share = jnp.sum(incoming[:, : share * width], axis=0).reshape(share, width)
    high = lax.reduce_precision(gram_share, 8, 7)
    low = gram_share - high
    pair = jnp.concatenate([high, low], axis=0).astype(jnp.bfloat16)
    located = jnp.concatenate(
        [
            token_factors[requests],
            jnp.broadcast_to(pair[None], (device_count, 2 * share, width)),
        ],
        axis=1,
    )
    fetched = lax.all_to_all(located, axes, split_axis=0, concat_axis=0, tiled=True)
    gram_matrix = (
        fetched[:, capacity : capacity + share].astype(jnp.float32)
        + fetched[:, capacity + share :].astype(jnp.float32)
    ).reshape(width, width)
    return pl.pallas_call(
        functools.partial(solve_body, capacity),
        out_shape=jax.ShapeDtypeStruct((host_count, width), jnp.float32),
        in_specs=[pl.BlockSpec(memory_space=pltpu.VMEM)] * 4,
        out_specs=pl.BlockSpec(memory_space=pltpu.VMEM),
        scratch_shapes=[pltpu.VMEM((host_count, width), jnp.float32)],
        compiler_params=pltpu.CompilerParams(vmem_limit_bytes=32 * 1024 * 1024),
    )(fetched, codes, gram_matrix, host_factors)


def solution(mesh):
    placed = (
        P(("parts", "shard", "sub"), None),
        P(("parts", "shard", "sub"), None),
        P(("parts", "shard", "sub"), None),
        P(("parts", "shard", "sub")),
        P(("parts", "shard", "sub"), None),
    )
    return jax.shard_map(
        shards,
        mesh=mesh,
        in_specs=placed,
        out_specs=P(("parts", "shard", "sub"), None),
        check_vma=False,
    )
```

time: 185 us -> 139 us (0.75)
  waiting for transfers between devices: 81.3 us -> 0 us
  blocking collectives: 13.6 us -> 76 us
  Pallas kernels: 0 us -> 35.4 us
  local copies, waits for them, and re-layouts: 41.7 us -> 16.8 us
  between operations: 13.8 us -> 0.19 us
  other arithmetic: 14.8 us -> 2.13 us
  matrix products: 15.3 us -> 8.13 us
  starting transfers between devices: 3.76 us -> 0 us
    all_to_all x1 -> x2, blocking collectives: 13.6 us -> 76 us  [the longest x1 58.4 us: shards(): lax.all_to_all(located, axes, split_axis=0, concat_axis=0, tiled=True)]
    all_to_all x1 -> x0, waiting for transfers between devices: 45.2 us -> none  [shards(): lax.all_to_all(located_rows, ('shard', 'sub'), split_axis=0, concat_axis=...]
    psum x1 -> x0, waiting for transfers between devices: 36 us -> none  [shards(): gram_matrix = lax.psum(partial_gram, ('shard', 'sub'))]
    pallas_call x0 -> x1, Pallas kernels: none -> 35.4 us  [shards(): pl.pallas_call(functools.partial(solve_body, capacity), out_shape=jax.Sha...]
    gather x2 -> x1, local copies, waits for them, and re-layouts: 35.5 us -> 15.7 us  [shards(): token_factors[requests]]
    unnamed x9 -> x2, other arithmetic: 10 us -> 0.01 us
    dot_general x5 -> x0, matrix products: 6.99 us -> none  [the longest x4 3.51 us: system_product(): jnp.dot(vectors, gram_matrix, precision=HIGHEST) + RIDGE_WEIGHT * vectors]
    all_to_all x1 -> x0, starting transfers between devices: 3.72 us -> none  [shards(): lax.all_to_all(located_rows, ('shard', 'sub'), split_axis=0, concat_axis=...]
  transfers between devices with their start and end apart: 2 -> 0, of which waited for: 2 -> 0; matrix products, arithmetic and copies ran while one was open for 17% -> 0% of each run, Pallas kernels for 0% -> 0%
where the time goes in v1:
time: 139 us
  blocking collectives  76 us (55%)
  Pallas kernels  35.4 us (25%)
  local copies, waits for them, and re-layouts  16.8 us (12%)
  matrix products  8.13 us (6%)
  other arithmetic  2.13 us (2%)
    all_to_all x1, blocking collectives, shards(): lax.all_to_all(located, axes, split_axis=0, concat_axis=0, tiled=True)  58.4 us
    pallas_call x1, Pallas kernels, shards(): pl.pallas_call(functools.partial(solve_body, capacity), out_shape=jax.Sha...  35.4 us
    all_to_all x1, blocking collectives, shards(): lax.all_to_all(outgoing, axes, split_axis=0, concat_axis=0, tiled=True)  17.6 us
    gather x1, local copies, waits for them, and re-layouts, shards(): token_factors[requests]  15.7 us
    dot_general x1, matrix products, shards(): lax.dot_general(token_factors, token_factors, (((0,), (0,)), ((), ())), p...  4.74 us
    dot_general x8, matrix products, place_block(): lax.dot_general(valued, rank_hot, (((0,), (0,)), ((), ())), precision=HIG...  2.92 us

profile of v1, /device:TPU:0, one launch (start us, length us, event | category | flops | bytes accessed | tf_op | source)
XLA Modules:
  0.0 139.1 jit_solution(14058450794141719945)
XLA Ops:
  0.0 0.7 add_select_fusion
  0.7 0.1 copy.12
  0.8 0.1 eq.34
  1.0 0.1 convert_reduce_fusion
  1.1 0.1 copy.13
  1.2 0.1 reshape_reshape.6
  1.3 0.7 broadcast_add_fusion
  2.1 0.1 copy.14
  2.2 0.1 reshape_reshape.7
  2.3 0.1 fusion.19
  2.4 0.3 fusion.9
  2.8 3.7 %while.11 = (s32[]{:T(128)}, f32[32,256]{1,0:T(8,128)S(1)}, bf16[8,512,17]{1,2,0:T(8,128)(2,1)S(1)}, s32[8,512]{1,0:T(8,128)S(1)}, s32[8,512]{1,0:T(8,128)S(1)}, /*index=5*/s32[8,512]{1,0:T(8,128)S(1)}, s32[]{:T(128)}, s32[]{:T(128)}) while((s32[]{:T(128)}, f32[32,256]{1,0:T(8,128)S(1)}, bf16[8,512,17]{1,2,0:T(8,128)(2,1)S(1)}, ...), condition=%wide.region_3.4_spmd.clone, body=%wide.region_2.3_spmd.clone.sunk | while | flops 50521088 | bytes 266355 | solution.py:71
  2.9 0.4 convolution_add_fusion.3
  3.3 0.4 convolution_add_fusion.3
  3.8 0.4 convolution_add_fusion.3
  4.3 0.4 convolution_add_fusion.3
  4.7 0.4 convolution_add_fusion.3
  5.2 0.4 convolution_add_fusion.3
  5.7 0.4 convolution_add_fusion.3
  6.1 0.4 convolution_add_fusion.3
  6.5 4.7 %fusion.20 = f32[256,256]{1,0:T(8,128)S(1)} fusion(bf16[8192,256]{1,0:T(8,128)(2,1)} %param.11), kind=kOutput, calls=%fused_computation.53 | convolution fusion | flops 1073741824 | bytes 4456448 | tf_op jit(solution)/shard_map/dot_general | solution.py:151
  11.3 0.1 reshape.71
  11.4 0.2 all_to_all.11
  11.6 17.6 %all_to_all.17 = f32[16,1,4352]{2,1,0:T(1,128)S(1)} all-to-all(f32[16,1,4352]{2,1,0:T(1,128)S(1)} %all_to_all.11), channel_id=1, replica_groups=mesh['parts'=2,'shard'=4,'sub'=4] {'shard','sub'}, dimensions={0} | all-to-all | bytes 557056 | tf_op jit(solution)/shard_map/all_to_all | solution.py:158
  29.3 15.7 %gather_fusion = bf16[4096,256]{1,0:T(8,128)(2,1)S(1)} fusion(bf16[8192,256]{1,0:T(8,128)(2,1)} %param.11, s32[4096]{0:T(1024)S(1)} %broadcast_clamp_fusion), kind=kCustom, calls=%fused_computation | custom fusion | bytes 4210688 | tf_op jit(solution)/shard_map/gather | solution.py:166
  45.1 0.2 pad_maximum_fusion
  45.3 0.0 copy-start
  45.3 58.4 %all_to_all.18.rows_ref = bf16[16,288,256]{2,1,0:T(8,128)(2,1)S(1)} all-to-all(bf16[16,288,256]{2,1,0:T(8,128)(2,1)S(1)} %pad_maximum_fusion), channel_id=1, replica_groups=mesh['parts'=2,'shard'=4,'sub'=4] {'shard','sub'}, dimensions={0} | all-to-all | bytes 4718592 | tf_op jit(solution)/shard_map/all_to_all | solution.py:171
  103.7 0.0 copy-done
  103.7 35.4 %shard_map.55 = f32[256,256]{1,0:T(8,128)} custom-call(bf16[16,288,256]{2,1,0:T(8,128)(2,1)S(1)} %all_to_all.18.rows_ref, s32[16,256]{1,0:T(8,128)S(1)} %get-tuple-element.88.code_ref, f32[256,256]{1,0:T(8,128)S(1)} %bitcast.33, f32[256,256]{1,0:T(8,128)S(1)} %copy-done), custom_call_target="tpu_custom_call" | custom-call | tf_op jit(solution)/shard_map/pallas_call | solution.py:176
  (48 shorter events, 0.6 us)
Async XLA Ops:
  45.3 58.4 %copy-start = (f32[256,256]{1,0:T(8,128)S(1)}, f32[256,256]{1,0:T(8,128)}, u32[]{:S(2)}) copy-start(f32[256,256]{1,0:T(8,128)} %start_ref.1) | copy-start | bytes 786436

commit v2 on v1

--- a/solution.py
+++ b/solution.py
@@ -87,49 +87,200 @@
     return jnp.concatenate([high, low], axis=0)
 
 
-def spread(capacity, rows_ref, code_ref, vectors, first, scratch_ref):
-    host_count = vectors.shape[0]
-    halves = split_pair(vectors)
-    scratch_ref[...] = jnp.zeros_like(scratch_ref)
-    row_host = lax.broadcasted_iota(jnp.int32, (host_count, capacity), 0) + 1
-
-    @pl.loop(0, rows_ref.shape[0])
-    def _(block):
-        rows = rows_ref[block, :capacity, :]
-        code = code_ref[pl.ds(block, 1), :]
+def solve_body(
+    sizes,
+    token_ref,
+    wanted_ref,
+    code_ref,
+    start_ref,
+    out_ref,
+    token_wide,
+    asked,
+    asked_scalar,
+    staged_wide,
+    staged,
+    fetched,
+    gram_own,
+    gram_parts,
+    gram_whole,
+    total_ref,
+    scalar_sem,
+    ask_send,
+    ask_recv,
+    part_send,
+    part_recv,
+    sum_send,
+    sum_recv,
+    row_send,
+    row_recv,
+):
+    outer, inner, capacity, group = sizes
+    count = outer * inner
+    owners, share, width = gram_whole.shape
+    at_outer, at_inner = lax.axis_index("shard"), lax.axis_index("sub")
+    me = at_outer * inner + at_inner
+
+    def partner(offset):
+        there_outer = lax.rem(at_outer + lax.rem(offset, outer), outer)
+        there_inner = lax.rem(at_inner + offset // outer, inner)
+        return there_outer * inner + there_inner, {"shard": there_outer, "sub": there_inner}
+
+    def each_partner(action):
+        @pl.loop(0, count - 1)
+        def _(step):
+            action(*partner(count - 1 - step))
+
+    def where_owner(device, action):
+        if owners == count:
+            action()
+        else:
+            pl.when(device < owners)(action)
+
+    def ask_copy(there, where, slot):
+        return pltpu.make_async_remote_copy(
+            src_ref=wanted_ref.at[there],
+            dst_ref=asked.at[slot],
+            send_sem=ask_send.at[there],
+            recv_sem=ask_recv.at[slot],
+            device_id=where,
+            device_id_type=pl.DeviceIdType.MESH,
+        )
+
+    def part_copy(there, where, slot):
+        return pltpu.make_async_remote_copy(
+            src_ref=gram_own.at[there],
+            dst_ref=gram_parts.at[slot],
+            send_sem=part_send.at[there],
+            recv_sem=part_recv.at[slot],
+            device_id=where,
+            device_id_type=pl.DeviceIdType.MESH,
+        )
+
+    def sum_copy(there, where, slot):
+        return pltpu.make_async_remote_copy(
+            src_ref=gram_whole.at[slot],
+            dst_ref=gram_whole.at[slot],
+            send_sem=sum_send.at[there],
+            recv_sem=sum_recv.at[slot],
+            device_id=where,
+            device_id_type=pl.DeviceIdType.MESH,
+        )
+
+    def row_copy(there, where, slot):
+        return pltpu.make_async_remote_copy(
+            src_ref=staged.at[there],
+            dst_ref=fetched.at[slot],
+            send_sem=row_send.at[there],
+            recv_sem=row_recv.at[slot],
+            device_id=where,
+            device_id_type=pl.DeviceIdType.MESH,
+        )
+
+    barrier = pltpu.get_barrier_semaphore()
+    each_partner(
+        lambda there, where: pl.semaphore_signal(
+            barrier, inc=1, device_id=where, device_id_type=pl.DeviceIdType.MESH
+        )
+    )
+    pl.semaphore_wait(barrier, count - 1)
+    each_partner(lambda there, where: ask_copy(there, where, me).start())
+
+    total_ref[...] = jnp.zeros_like(total_ref)
+    strip = math.gcd(token_ref.shape[0], 1024)
+
+    @pl.loop(0, token_ref.shape[0] // strip)
+    def _(index):
+        at = pl.ds(pl.multiple_of(index * strip, strip), strip)
+        rows = token_ref[at, :]
+        token_wide[at, :] = rows.astype(jnp.float32)
+        total_ref[...] += lax.dot_general(
+            rows, rows, (((0,), (0,)), ((), ())), preferred_element_type=jnp.float32
+        )
+
+    gram_own[...] = total_ref[...].reshape(owners, share, width)
+    each_partner(
+        lambda there, where: where_owner(there, lambda: part_copy(there, where, me).start())
+    )
+
+    each_partner(lambda there, where: ask_copy(there, where, there).wait_recv())
+    asked[pl.ds(me, 1)] = wanted_ref[pl.ds(me, 1)]
+    to_scalar = pltpu.make_async_copy(asked, asked_scalar, scalar_sem)
+    to_scalar.start()
+    to_scalar.wait()
+
+    def collect(there, target):
+        burst = math.gcd(capacity, 32)
+
+        @pl.loop(0, capacity // burst)
+        def _(index):
+            first = pl.multiple_of(index * burst, burst)
+            for row in range(burst):
+                chosen = asked_scalar[there, 0, first + row]
+                staged_wide[pl.ds(first + row, 1), :] = token_wide[pl.ds(chosen, 1), :]
+
+        target[there] = staged_wide[...].astype(jnp.bfloat16)
+
+    def serve(there, where):
+        collect(there, staged)
+        row_copy(there, where, me).start()
+
+    each_partner(serve)
+    collect(me, fetched)
+
+    def reduce_part():
+        gram_parts[pl.ds(me, 1)] = gram_own[pl.ds(me, 1)]
+        each_partner(lambda there, where: part_copy(me, where, there).wait_recv())
+        gram_whole[pl.ds(me, 1)] = jnp.sum(gram_parts[...], axis=0, keepdims=True)
+        each_partner(lambda there, where: sum_copy(there, where, me).start())
+
+    where_owner(me, reduce_part)
+
+    host_count = start_ref.shape[0]
+    row_host = lax.broadcasted_iota(jnp.int32, (host_count, group * capacity), 0) + 1
+
+    def inner_products(index, halves):
+        rows = fetched[pl.ds(index * group, group)].reshape(group * capacity, width)
         both = lax.dot_general(
             halves, rows, (((1,), (1,)), ((), ())), preferred_element_type=jnp.float32
         )
-        inner = both[:host_count] + both[host_count:]
+        code = code_ref[index]
         weight = CONFIDENCE_SCALE * (code % COUNT_SPAN).astype(jnp.float32)
-        if first:
-            value = (1.0 + weight) - weight * inner
-        else:
-            value = weight * inner
-        masked = jnp.where(row_host == code // COUNT_SPAN, value, 0.0)
+        return rows, both[:host_count] + both[host_count:], row_host == code // COUNT_SPAN, weight
+
+    def add_rows(masked, rows):
         out = jnp.dot(split_pair(masked), rows, preferred_element_type=jnp.float32)
-        scratch_ref[...] += out[:host_count] + out[host_count:]
-
-    return scratch_ref[...]
-
-
-def solve_body(capacity, rows_ref, code_ref, gram_ref, start_ref, out_ref, scratch_ref):
+        total_ref[...] += out[:host_count] + out[host_count:]
+
+    def spread(vectors, first):
+        halves = split_pair(vectors)
+        total_ref[...] = jnp.zeros_like(total_ref)
+
+        @pl.loop(0, count // group)
+        def _(index):
+            rows, product, own, weight = inner_products(index, halves)
+            value = (1.0 + weight) - weight * product if first else weight * product
+            add_rows(jnp.where(own, value, 0.0), rows)
+
+        return total_ref[...]
+
     def smooth(vectors):
+        gram = gram_whole[...].reshape(width, width)
         return (
-            jnp.dot(
-                vectors, gram_ref[...], precision=HIGHEST, preferred_element_type=jnp.float32
-            )
+            jnp.dot(vectors, gram, precision=HIGHEST, preferred_element_type=jnp.float32)
             + RIDGE_WEIGHT * vectors
         )
 
+    each_partner(lambda there, where: row_copy(there, where, there).wait_recv())
     iterate = start_ref[...]
-    residual = spread(capacity, rows_ref, code_ref, iterate, True, scratch_ref) - smooth(iterate)
+    residual = spread(iterate, True)
+    each_partner(
+        lambda there, where: where_owner(there, lambda: sum_copy(there, where, there).wait_recv())
+    )
+    residual = residual - smooth(iterate)
     direction = residual
     norm_now = jnp.sum(residual * residual, axis=1, keepdims=True)
     for iteration in range(CG_STEPS):
-        image = spread(capacity, rows_ref, code_ref, direction, False, scratch_ref) + smooth(
-            direction
-        )
+        image = spread(direction, False) + smooth(direction)
         step_size = norm_now / (jnp.sum(direction * image, axis=1, keepdims=True) + SMALL_EPSILON)
         iterate = iterate + step_size * direction
         if iteration < CG_STEPS - 1:
@@ -139,48 +290,55 @@
             norm_now = norm_next
     out_ref[...] = iterate
 
+    def settle(there, where):
+        ask_copy(there, where, me).wait_send()
+        where_owner(there, lambda: part_copy(there, where, me).wait_send())
+        where_owner(me, lambda: sum_copy(there, where, me).wait_send())
+        row_copy(there, where, me).wait_send()
+
+    each_partner(settle)
+
 
 def shards(host_factors, token_ids, counts, lengths, token_factors):
-    axes = ("shard", "sub")
-    device_count = lax.axis_size(axes)
+    outer, inner = lax.axis_size("shard"), lax.axis_size("sub")
+    device_count = outer * inner
     token_rows = token_factors.shape[0]
     host_count, slot_count = token_ids.shape
     width = host_factors.shape[1]
-    capacity = max(4, host_count * slot_count // device_count)
-    share = width // device_count
-    partial_gram = lax.dot_general(
-        token_factors, token_factors, (((0,), (0,)), ((), ())), preferred_element_type=jnp.float32
-    )
+    capacity = max(16, host_count * slot_count // device_count)
+    share = max(8, width // device_count)
+    owners = width // share
+    group = math.gcd(device_count, max(1, 1024 // capacity))
     wanted, codes = request_tables(
         token_ids, counts, lengths, token_rows, device_count, capacity
     )
-    outgoing = jnp.concatenate([partial_gram.reshape(device_count, share * width), wanted], axis=1)
-    incoming = lax.all_to_all(outgoing, axes, split_axis=0, concat_axis=0, tiled=True)
-    requests = incoming[:, share * width :].astype(jnp.int32)
-    gram_share = jnp.sum(incoming[:, : share * width], axis=0).reshape(share, width)
-    high = lax.reduce_precision(gram_share, 8, 7)
-    low = gram_share - high
-    pair = jnp.concatenate([high, low], axis=0).astype(jnp.bfloat16)
-    located = jnp.concatenate(
-        [
-            token_factors[requests],
-            jnp.broadcast_to(pair[None], (device_count, 2 * share, width)),
-        ],
-        axis=1,
-    )
-    fetched = lax.all_to_all(located, axes, split_axis=0, concat_axis=0, tiled=True)
-    gram_matrix = (
-        fetched[:, capacity : capacity + share].astype(jnp.float32)
-        + fetched[:, capacity + share :].astype(jnp.float32)
-    ).reshape(width, width)
+    wanted = wanted.astype(jnp.int32).reshape(device_count, 1, capacity)
+    codes = codes.reshape(device_count // group, 1, group * capacity)
+    in_vmem = pl.BlockSpec(memory_space=pltpu.VMEM)
+    links = [pltpu.SemaphoreType.DMA((device_count,))] * 8
     return pl.pallas_call(
-        functools.partial(solve_body, capacity),
+        functools.partial(solve_body, (outer, inner, capacity, group)),
         out_shape=jax.ShapeDtypeStruct((host_count, width), jnp.float32),
-        in_specs=[pl.BlockSpec(memory_space=pltpu.VMEM)] * 4,
-        out_specs=pl.BlockSpec(memory_space=pltpu.VMEM),
-        scratch_shapes=[pltpu.VMEM((host_count, width), jnp.float32)],
-        compiler_params=pltpu.CompilerParams(vmem_limit_bytes=32 * 1024 * 1024),
-    )(fetched, codes, gram_matrix, host_factors)
+        in_specs=[in_vmem] * 4,
+        out_specs=in_vmem,
+        scratch_shapes=[
+            pltpu.VMEM((token_rows, width), jnp.float32),
+            pltpu.VMEM((device_count, 1, capacity), jnp.int32),
+            pltpu.SMEM((device_count, 1, capacity), jnp.int32),
+            pltpu.VMEM((capacity, width), jnp.float32),
+            pltpu.VMEM((device_count, capacity, width), jnp.bfloat16),
+            pltpu.VMEM((device_count, capacity, width), jnp.bfloat16),
+            pltpu.VMEM((owners, share, width), jnp.float32),
+            pltpu.VMEM((device_count, share, width), jnp.float32),
+            pltpu.VMEM((owners, share, width), jnp.float32),
+            pltpu.VMEM((host_count, width), jnp.float32),
+            pltpu.SemaphoreType.DMA,
+        ]
+        + links,
+        compiler_params=pltpu.CompilerParams(
+            vmem_limit_bytes=48 * 1024 * 1024, collective_id=0, has_side_effects=True
+        ),
+    )(token_factors, wanted, codes, host_factors)
 
 
 def solution(mesh):

time: 139 us -> 93.2 us (0.67)
  blocking collectives: 76 us -> 0 us
  Pallas kernels: 35.4 us -> 83.4 us
  local copies, waits for them, and re-layouts: 16.8 us -> 3.74 us
  matrix products: 8.13 us -> 3.39 us
    all_to_all x2 -> x0, blocking collectives: 76 us -> none  [the longest x1 58.4 us: shards(): lax.all_to_all(located, axes, split_axis=0, concat_axis=0, tiled=True)]
    pallas_call x1, Pallas kernels: 35.4 us -> 83.4 us  [shards(): pl.pallas_call(functools.partial(solve_body, (outer, inner, capacity, gro...]
    gather x1 -> x0, local copies, waits for them, and re-layouts: 15.7 us -> none  [shards(): token_factors[requests]]
    dot_general x1 -> x0, matrix products: 4.74 us -> none  [shards(): lax.dot_general(token_factors, token_factors, (((0,), (0,)), ((), ())), p...]
    unnamed x4 -> x5, local copies, waits for them, and re-layouts: 0.04 us -> 2.89 us
where the time goes in v2:
time: 93.2 us; the launch traced here: 92.9 us
  Pallas kernels  83.4 us (89%)
  local copies, waits for them, and re-layouts  3.74 us (4%)
  matrix products  3.39 us (4%)
  other arithmetic  1.86 us (2%)
    pallas_call x1, Pallas kernels, shards(): pl.pallas_call(functools.partial(solve_body, (outer, inner, capacity, gro...  83.4 us
    dot_general x8, matrix products, place_block(): lax.dot_general(valued, rank_hot, (((0,), (0,)), ((), ())), precision=HIG...  2.92 us
    unnamed x5, local copies, waits for them, and re-layouts  2.89 us

profile of v2, /device:TPU:0, one launch (start us, length us, event | category | flops | bytes accessed | tf_op | source)
XLA Modules:
  0.0 92.9 jit_solution(11085377395899939776)
XLA Ops:
  0.0 0.0 copy-start.1
  0.0 0.8 broadcast_add_fusion
  0.8 0.7 add_select_fusion
  1.5 0.1 copy.10
  1.6 0.1 reshape_reshape.6
  1.7 0.1 copy.11
  1.8 0.1 reshape_reshape.7
  1.9 0.1 copy.9
  2.0 0.1 eq.34
  2.2 0.1 convert_reduce_fusion
  2.3 0.1 fusion.17
  2.4 0.4 fusion.9
  2.8 3.7 %while.11 = (s32[]{:T(128)}, f32[32,256]{1,0:T(8,128)S(1)}, bf16[8,512,17]{1,2,0:T(8,128)(2,1)S(1)}, s32[8,512]{1,0:T(8,128)S(1)}, s32[8,512]{1,0:T(8,128)S(1)}, /*index=5*/s32[8,512]{1,0:T(8,128)S(1)}, s32[]{:T(128)}, s32[]{:T(128)}) while((s32[]{:T(128)}, f32[32,256]{1,0:T(8,128)S(1)}, bf16[8,512,17]{1,2,0:T(8,128)(2,1)S(1)}, ...), condition=%wide.region_3.4_spmd.clone, body=%wide.region_2.3_spmd.clone.sunk | while | flops 50521088 | bytes 266355 | solution.py:71
  2.9 0.4 convolution_add_fusion.3
  3.4 0.4 convolution_add_fusion.3
  3.8 0.4 convolution_add_fusion.3
  4.3 0.4 convolution_add_fusion.3
  4.8 0.4 convolution_add_fusion.3
  5.2 0.4 convolution_add_fusion.3
  5.7 0.4 convolution_add_fusion.3
  6.2 0.4 convolution_add_fusion.3
  6.6 0.0 copy-done.1
  6.6 0.0 copy-start
  6.6 2.2 %copy-done = bf16[8192,256]{1,0:T(8,128)(2,1)S(1)} copy-done((bf16[8192,256]{1,0:T(8,128)(2,1)S(1)}, bf16[8192,256]{1,0:T(8,128)(2,1)}, u32[]{:S(2)}) %copy-start) | copy-done | bytes 4194328
  8.8 83.4 %shard_map.55 = f32[256,256]{1,0:T(8,128)S(1)} custom-call(bf16[8192,256]{1,0:T(8,128)(2,1)S(1)} %copy-done, s32[16,1,256]{2,1,0:T(1,128)S(1)} %reshape.51.wanted_ref, s32[4,1,1024]{2,1,0:T(1,128)S(1)} %reshape.52.code_ref, f32[256,256]{1,0:T(8,128)S(1)} %copy-done.1), custom_call_target="tpu_custom_call" | custom-call | tf_op jit(solution)/shard_map/pallas_call | solution.py:319
  92.2 0.7 copy.19
  (39 shorter events, 0.5 us)
Async XLA Ops:
  0.0 6.6 %copy-start.1 = (f32[256,256]{1,0:T(8,128)S(1)}, f32[256,256]{1,0:T(8,128)}, u32[]{:S(2)}) copy-start(f32[256,256]{1,0:T(8,128)} %start_ref.1) | copy-start | bytes 786436
  6.6 2.2 %copy-start = (bf16[8192,256]{1,0:T(8,128)(2,1)S(1)}, bf16[8192,256]{1,0:T(8,128)(2,1)}, u32[]{:S(2)}) copy-start(bf16[8192,256]{1,0:T(8,128)(2,1)} %token_ref.1) | copy-start | bytes 12582916

commit v3 on v2

--- a/solution.py
+++ b/solution.py
@@ -14,6 +14,7 @@
 SMALL_EPSILON = 1e-06
 HIGHEST = lax.Precision.HIGHEST
 COUNT_SPAN = 64
+DIGIT = 128
 
 
 def owner_ranks(owner_hot, block_rows):
@@ -41,44 +42,24 @@
     codes = ((hosts + 1) * COUNT_SPAN + counts).reshape(-1)
     total_rows = host_count * slot_count
     block_rows = math.gcd(total_rows, 512)
-    block_count = total_rows // block_rows
     owner_hot = (owners[:, None] == jnp.arange(device_count + 1, dtype=jnp.int32)[None, :]).astype(
         jnp.bfloat16
     )
     ranks = owner_ranks(owner_hot, block_rows)
     capacity_index = jnp.arange(capacity, dtype=jnp.int32)
 
-    def place_block(total, packed):
-        hot_block, row_block, code_block, rank_block = packed
-        hot = hot_block[:, :device_count].astype(jnp.float32)
-        valued = jnp.concatenate(
-            [
-                hot * row_block.astype(jnp.float32)[:, None],
-                hot * code_block.astype(jnp.float32)[:, None],
-            ],
-            axis=1,
-        )
-        rank_hot = (rank_block[:, None] == capacity_index[None, :]).astype(jnp.float32)
-        placed = lax.dot_general(
-            valued,
-            rank_hot,
-            (((0,), (0,)), ((), ())),
-            precision=HIGHEST,
-            preferred_element_type=jnp.float32,
-        )
-        return (total + placed, None)
-
-    tables, unused = lax.scan(
-        place_block,
-        jnp.zeros((2 * device_count, capacity), jnp.float32),
-        (
-            owner_hot.reshape(block_count, block_rows, device_count + 1),
-            local_rows.reshape(block_count, block_rows),
-            codes.reshape(block_count, block_rows),
-            ranks.reshape(block_count, block_rows),
-        ),
-    )
-    return tables[:device_count], tables[device_count:].astype(jnp.int32)
+    digits = jnp.stack(
+        [local_rows // DIGIT, local_rows % DIGIT, codes // DIGIT, codes % DIGIT], axis=1
+    ).astype(jnp.bfloat16)
+    valued = (digits[:, :, None] * owner_hot[:, None, :device_count]).reshape(
+        total_rows, 4 * device_count
+    )
+    rank_hot = (ranks[:, None] == capacity_index[None, :]).astype(jnp.bfloat16)
+    placed = lax.dot_general(
+        valued, rank_hot, (((0,), (0,)), ((), ())), preferred_element_type=jnp.float32
+    )
+    placed = placed.astype(jnp.int32).reshape(4, device_count, capacity)
+    return placed[0] * DIGIT + placed[1], placed[2] * DIGIT + placed[3]
 
 
 def split_pair(values):
@@ -114,19 +95,21 @@
     row_send,
     row_recv,
 ):
-    outer, inner, capacity, group = sizes
+    outer, inner, capacity = sizes
+    group = outer
     count = outer * inner
     owners, share, width = gram_whole.shape
     at_outer, at_inner = lax.axis_index("shard"), lax.axis_index("sub")
     me = at_outer * inner + at_inner
+    my_place = at_inner * outer + at_outer
 
     def partner(offset):
         there_outer = lax.rem(at_outer + lax.rem(offset, outer), outer)
         there_inner = lax.rem(at_inner + offset // outer, inner)
         return there_outer * inner + there_inner, {"shard": there_outer, "sub": there_inner}
 
-    def each_partner(action):
-        @pl.loop(0, count - 1)
+    def each_partner(action, first=0, last=count - 1):
+        @pl.loop(first, last)
         def _(step):
             action(*partner(count - 1 - step))
 
@@ -185,22 +168,12 @@
     pl.semaphore_wait(barrier, count - 1)
     each_partner(lambda there, where: ask_copy(there, where, me).start())
 
-    total_ref[...] = jnp.zeros_like(total_ref)
     strip = math.gcd(token_ref.shape[0], 1024)
 
     @pl.loop(0, token_ref.shape[0] // strip)
     def _(index):
         at = pl.ds(pl.multiple_of(index * strip, strip), strip)
-        rows = token_ref[at, :]
-        token_wide[at, :] = rows.astype(jnp.float32)
-        total_ref[...] += lax.dot_general(
-            rows, rows, (((0,), (0,)), ((), ())), preferred_element_type=jnp.float32
-        )
-
-    gram_own[...] = total_ref[...].reshape(owners, share, width)
-    each_partner(
-        lambda there, where: where_owner(there, lambda: part_copy(there, where, me).start())
-    )
+        token_wide[at, :] = token_ref[at, :].astype(jnp.float32)
 
     each_partner(lambda there, where: ask_copy(there, where, there).wait_recv())
     asked[pl.ds(me, 1)] = wanted_ref[pl.ds(me, 1)]
@@ -208,7 +181,7 @@
     to_scalar.start()
     to_scalar.wait()
 
-    def collect(there, target):
+    def collect(there, target, place):
         burst = math.gcd(capacity, 32)
 
         @pl.loop(0, capacity // burst)
@@ -218,14 +191,30 @@
                 chosen = asked_scalar[there, 0, first + row]
                 staged_wide[pl.ds(first + row, 1), :] = token_wide[pl.ds(chosen, 1), :]
 
-        target[there] = staged_wide[...].astype(jnp.bfloat16)
+        target[place] = staged_wide[...].astype(jnp.bfloat16)
 
     def serve(there, where):
-        collect(there, staged)
-        row_copy(there, where, me).start()
-
-    each_partner(serve)
-    collect(me, fetched)
+        collect(there, staged, there)
+        row_copy(there, where, my_place).start()
+
+    half = count // 2
+    each_partner(serve, 0, half)
+
+    total_ref[...] = jnp.zeros_like(total_ref)
+
+    @pl.loop(0, token_ref.shape[0] // strip)
+    def _(index):
+        rows = token_ref[pl.ds(pl.multiple_of(index * strip, strip), strip), :]
+        total_ref[...] += lax.dot_general(
+            rows, rows, (((0,), (0,)), ((), ())), preferred_element_type=jnp.float32
+        )
+
+    gram_own[...] = total_ref[...].reshape(owners, share, width)
+    each_partner(
+        lambda there, where: where_owner(there, lambda: part_copy(there, where, me).start())
+    )
+    each_partner(serve, half, count - 1)
+    collect(me, fetched, my_place)
 
     def reduce_part():
         gram_parts[pl.ds(me, 1)] = gram_own[pl.ds(me, 1)]
@@ -251,17 +240,55 @@
         out = jnp.dot(split_pair(masked), rows, preferred_element_type=jnp.float32)
         total_ref[...] += out[:host_count] + out[host_count:]
 
-    def spread(vectors, first):
+    def first_spread(vectors):
         halves = split_pair(vectors)
         total_ref[...] = jnp.zeros_like(total_ref)
 
-        @pl.loop(0, count // group)
+        def arrive(index, source):
+            where = {"shard": source, "sub": index}
+            row_copy(source * inner + index, where, index * outer + source).wait_recv()
+
+        def add_group(index):
+            rows, product, own, weight = inner_products(index, halves)
+            add_rows(jnp.where(own, (1.0 + weight) - weight * product, 0.0), rows)
+
+        @pl.loop(0, inner - 1)
+        def _(step):
+            index = lax.rem(at_inner + 1 + step, inner)
+
+            @pl.loop(0, outer)
+            def _(source):
+                arrive(index, source)
+
+            add_group(index)
+
+        @pl.loop(0, outer - 1)
+        def _(step):
+            arrive(at_inner, lax.rem(at_outer + 1 + step, outer))
+
+        add_group(at_inner)
+        return total_ref[...]
+
+    def spread(vectors):
+        halves = split_pair(vectors)
+        total_ref[...] = jnp.zeros_like(total_ref)
+
+        @pl.loop(0, inner)
         def _(index):
             rows, product, own, weight = inner_products(index, halves)
-            value = (1.0 + weight) - weight * product if first else weight * product
-            add_rows(jnp.where(own, value, 0.0), rows)
+            add_rows(jnp.where(own, weight * product, 0.0), rows)
 
         return total_ref[...]
+
+    def squares(vectors):
+        halves = split_pair(vectors)
+
+        def add(index, total):
+            rows, product, own, weight = inner_products(index, halves)
+            value = jnp.where(own, weight * product * product, 0.0)
+            return total + jnp.sum(value, axis=1, keepdims=True)
+
+        return lax.fori_loop(0, inner, add, jnp.zeros((host_count, 1), jnp.float32))
 
     def smooth(vectors):
         gram = gram_whole[...].reshape(width, width)
@@ -270,9 +297,8 @@
             + RIDGE_WEIGHT * vectors
         )
 
-    each_partner(lambda there, where: row_copy(there, where, there).wait_recv())
     iterate = start_ref[...]
-    residual = spread(iterate, True)
+    residual = first_spread(iterate)
     each_partner(
         lambda there, where: where_owner(there, lambda: sum_copy(there, where, there).wait_recv())
     )
@@ -280,8 +306,13 @@
     direction = residual
     norm_now = jnp.sum(residual * residual, axis=1, keepdims=True)
     for iteration in range(CG_STEPS):
-        image = spread(direction, False) + smooth(direction)
-        step_size = norm_now / (jnp.sum(direction * image, axis=1, keepdims=True) + SMALL_EPSILON)
+        image = smooth(direction)
+        if iteration < CG_STEPS - 1:
+            image = image + spread(direction)
+            along = jnp.sum(direction * image, axis=1, keepdims=True)
+        else:
+            along = jnp.sum(direction * image, axis=1, keepdims=True) + squares(direction)
+        step_size = norm_now / (along + SMALL_EPSILON)
         iterate = iterate + step_size * direction
         if iteration < CG_STEPS - 1:
             residual = residual - step_size * image
@@ -294,7 +325,7 @@
         ask_copy(there, where, me).wait_send()
         where_owner(there, lambda: part_copy(there, where, me).wait_send())
         where_owner(me, lambda: sum_copy(there, where, me).wait_send())
-        row_copy(there, where, me).wait_send()
+        row_copy(there, where, my_place).wait_send()
 
     each_partner(settle)
 
@@ -308,16 +339,16 @@
     capacity = max(16, host_count * slot_count // device_count)
     share = max(8, width // device_count)
     owners = width // share
-    group = math.gcd(device_count, max(1, 1024 // capacity))
     wanted, codes = request_tables(
         token_ids, counts, lengths, token_rows, device_count, capacity
     )
-    wanted = wanted.astype(jnp.int32).reshape(device_count, 1, capacity)
-    codes = codes.reshape(device_count // group, 1, group * capacity)
+    wanted = wanted.reshape(device_count, 1, capacity)
+    codes = codes.reshape(outer, inner, capacity).transpose(1, 0, 2)
+    codes = codes.reshape(inner, 1, outer * capacity)
     in_vmem = pl.BlockSpec(memory_space=pltpu.VMEM)
     links = [pltpu.SemaphoreType.DMA((device_count,))] * 8
     return pl.pallas_call(
-        functools.partial(solve_body, (outer, inner, capacity, group)),
+        functools.partial(solve_body, (outer, inner, capacity)),
         out_shape=jax.ShapeDtypeStruct((host_count, width), jnp.float32),
         in_specs=[in_vmem] * 4,
         out_specs=in_vmem,

time: 93.2 us -> 93.4 us (level)
  Pallas kernels: 83.4 us -> 85.8 us
  matrix products: 3.39 us -> 1.34 us
    pallas_call x1, Pallas kernels: 83.4 us -> 85.8 us  [shards(): pl.pallas_call(functools.partial(solve_body, (outer, inner, capacity)), o...]
    dot_general x8 -> x1, matrix products: 2.92 us -> 0.87 us  [request_tables(): lax.dot_general(valued, rank_hot, (((0,), (0,)), ((), ())), preferred_ele...]
    unnamed x5 -> x6, local copies, waits for them, and re-layouts: 2.89 us -> 2.9 us
where the time goes in v3:
time: 93.4 us; the launch traced here: 93 us
  Pallas kernels  85.8 us (92%)
  local copies, waits for them, and re-layouts  3.69 us (4%)
  other arithmetic  2.04 us (2%)
  matrix products  1.34 us (1%)
    pallas_call x1, Pallas kernels, shards(): pl.pallas_call(functools.partial(solve_body, (outer, inner, capacity)), o...  85.8 us
    unnamed x6, local copies, waits for them, and re-layouts  2.9 us

profile of v3, /device:TPU:0, one launch (start us, length us, event | category | flops | bytes accessed | tf_op | source)
XLA Modules:
  0.0 93.0 jit_solution(11754608694362564076)
XLA Ops:
  0.0 0.0 copy-start.1
  0.0 0.8 broadcast_add_fusion
  0.8 0.7 add_select_fusion.1
  1.5 0.1 copy.7
  1.6 0.1 reshape.321
  1.7 0.1 fusion.15
  1.8 0.1 copy.8
  1.9 0.1 reshape.322
  2.0 0.1 fusion.16
  2.1 0.1 fusion.12
  2.2 0.1 pad_maximum_fusion
  2.3 0.1 copy.9
  2.4 0.1 eq.47
  2.5 0.1 eq.43
  2.6 0.1 convert_reduce_fusion
  2.7 0.1 fusion.18
  2.9 0.3 fusion.4
  3.3 0.1 broadcast_multiply_fusion
  3.3 0.9 fusion.5
  4.3 0.0 copy-done.1
  4.3 0.0 copy-start
  4.3 2.2 %copy-done = bf16[8192,256]{1,0:T(8,128)(2,1)S(1)} copy-done((bf16[8192,256]{1,0:T(8,128)(2,1)S(1)}, bf16[8192,256]{1,0:T(8,128)(2,1)}, u32[]{:S(2)}) %copy-start) | copy-done | bytes 4194328
  6.5 85.8 %shard_map.55 = f32[256,256]{1,0:T(8,128)S(1)} custom-call(bf16[8192,256]{1,0:T(8,128)(2,1)S(1)} %copy-done, s32[16,1,256]{2,1,0:T(1,128)S(1)} %add.110.wanted_ref, s32[4,1,1024]{2,1,0:T(1,128)S(1)} %reshape.323.code_ref, f32[256,256]{1,0:T(8,128)S(1)} %copy-done.1), custom_call_target="tpu_custom_call" | custom-call | tf_op jit(solution)/shard_map/pallas_call | solution.py:350
  92.3 0.7 copy.16
  (9 shorter events, 0.1 us)
Async XLA Ops:
  0.0 4.3 %copy-start.1 = (f32[256,256]{1,0:T(8,128)S(1)}, f32[256,256]{1,0:T(8,128)}, u32[]{:S(2)}) copy-start(f32[256,256]{1,0:T(8,128)} %start_ref.1) | copy-start | bytes 786436
  4.3 2.2 %copy-start = (bf16[8192,256]{1,0:T(8,128)(2,1)S(1)}, bf16[8192,256]{1,0:T(8,128)(2,1)}, u32[]{:S(2)}) copy-start(bf16[8192,256]{1,0:T(8,128)(2,1)} %token_ref.1) | copy-start | bytes 12582916

commit v4 on v3

--- a/solution.py
+++ b/solution.py
@@ -108,8 +108,8 @@
         there_inner = lax.rem(at_inner + offset // outer, inner)
         return there_outer * inner + there_inner, {"shard": there_outer, "sub": there_inner}
 
-    def each_partner(action, first=0, last=count - 1):
-        @pl.loop(first, last)
+    def each_partner(action):
+        @pl.loop(0, count - 1)
         def _(step):
             action(*partner(count - 1 - step))
 
@@ -168,12 +168,22 @@
     pl.semaphore_wait(barrier, count - 1)
     each_partner(lambda there, where: ask_copy(there, where, me).start())
 
-    strip = math.gcd(token_ref.shape[0], 1024)
+    total_ref[...] = jnp.zeros_like(total_ref)
+    strip = math.gcd(token_ref.shape[0], 2048)
 
     @pl.loop(0, token_ref.shape[0] // strip)
     def _(index):
         at = pl.ds(pl.multiple_of(index * strip, strip), strip)
-        token_wide[at, :] = token_ref[at, :].astype(jnp.float32)
+        rows = token_ref[at, :]
+        token_wide[at, :] = rows.astype(jnp.float32)
+        total_ref[...] += lax.dot_general(
+            rows, rows, (((0,), (0,)), ((), ())), preferred_element_type=jnp.float32
+        )
+
+    gram_own[...] = total_ref[...].reshape(owners, share, width)
+    each_partner(
+        lambda there, where: where_owner(there, lambda: part_copy(there, where, me).start())
+    )
 
     each_partner(lambda there, where: ask_copy(there, where, there).wait_recv())
     asked[pl.ds(me, 1)] = wanted_ref[pl.ds(me, 1)]
@@ -197,23 +207,7 @@
         collect(there, staged, there)
         row_copy(there, where, my_place).start()
 
-    half = count // 2
-    each_partner(serve, 0, half)
-
-    total_ref[...] = jnp.zeros_like(total_ref)
-
-    @pl.loop(0, token_ref.shape[0] // strip)
-    def _(index):
-        rows = token_ref[pl.ds(pl.multiple_of(index * strip, strip), strip), :]
-        total_ref[...] += lax.dot_general(
-            rows, rows, (((0,), (0,)), ((), ())), preferred_element_type=jnp.float32
-        )
-
-    gram_own[...] = total_ref[...].reshape(owners, share, width)
-    each_partner(
-        lambda there, where: where_owner(there, lambda: part_copy(there, where, me).start())
-    )
-    each_partner(serve, half, count - 1)
+    each_partner(serve)
     collect(me, fetched, my_place)
 
     def reduce_part():

time: 93.4 us -> 88.2 us (0.944)
  Pallas kernels: 85.8 us -> 80.6 us
    pallas_call x1, Pallas kernels: 85.8 us -> 80.6 us  [shards(): pl.pallas_call(functools.partial(solve_body, (outer, inner, capacity)), o...]
where the time goes in v4:
time: 88.2 us; the launch traced here: 87.8 us
  Pallas kernels  80.6 us (91%)
  local copies, waits for them, and re-layouts  3.69 us (4%)
  other arithmetic  2.04 us (2%)
  matrix products  1.34 us (2%)
    pallas_call x1, Pallas kernels, shards(): pl.pallas_call(functools.partial(solve_body, (outer, inner, capacity)), o...  80.6 us
    unnamed x6, local copies, waits for them, and re-layouts  2.9 us

profile of v4, /device:TPU:0, one launch (start us, length us, event | category | flops | bytes accessed | tf_op | source)
XLA Modules:
  0.0 87.8 jit_solution(3273216535950708300)
XLA Ops:
  0.0 0.0 copy-start.1
  0.0 0.8 broadcast_add_fusion
  0.8 0.7 add_select_fusion.1
  1.5 0.1 copy.7
  1.6 0.1 reshape.321
  1.7 0.1 fusion.15
  1.8 0.1 copy.8
  1.9 0.1 reshape.322
  2.0 0.1 fusion.16
  2.1 0.1 fusion.12
  2.2 0.1 pad_maximum_fusion
  2.3 0.1 copy.9
  2.4 0.1 eq.47
  2.5 0.1 eq.43
  2.6 0.1 convert_reduce_fusion
  2.7 0.1 fusion.18
  2.9 0.3 fusion.4
  3.3 0.1 broadcast_multiply_fusion
  3.3 0.9 fusion.5
  4.3 0.0 copy-done.1
  4.3 0.0 copy-start
  4.3 2.2 %copy-done = bf16[8192,256]{1,0:T(8,128)(2,1)S(1)} copy-done((bf16[8192,256]{1,0:T(8,128)(2,1)S(1)}, bf16[8192,256]{1,0:T(8,128)(2,1)}, u32[]{:S(2)}) %copy-start) | copy-done | bytes 4194328
  6.5 80.6 %shard_map.55 = f32[256,256]{1,0:T(8,128)S(1)} custom-call(bf16[8192,256]{1,0:T(8,128)(2,1)S(1)} %copy-done, s32[16,1,256]{2,1,0:T(1,128)S(1)} %add.110.wanted_ref, s32[4,1,1024]{2,1,0:T(1,128)S(1)} %reshape.323.code_ref, f32[256,256]{1,0:T(8,128)S(1)} %copy-done.1), custom_call_target="tpu_custom_call" | custom-call | tf_op jit(solution)/shard_map/pallas_call | solution.py:344
  87.1 0.7 copy.16
  (9 shorter events, 0.1 us)
Async XLA Ops:
  0.0 4.3 %copy-start.1 = (f32[256,256]{1,0:T(8,128)S(1)}, f32[256,256]{1,0:T(8,128)}, u32[]{:S(2)}) copy-start(f32[256,256]{1,0:T(8,128)} %start_ref.1) | copy-start | bytes 786436
  4.3 2.2 %copy-start = (bf16[8192,256]{1,0:T(8,128)(2,1)S(1)}, bf16[8192,256]{1,0:T(8,128)(2,1)}, u32[]{:S(2)}) copy-start(bf16[8192,256]{1,0:T(8,128)(2,1)} %token_ref.1) | copy-start | bytes 12582916

commit v5 on v4

--- a/solution.py
+++ b/solution.py
@@ -70,11 +70,12 @@
 
 def solve_body(
     sizes,
-    token_ref,
+    token_home,
     wanted_ref,
     code_ref,
     start_ref,
     out_ref,
+    token_ref,
     token_wide,
     asked,
     asked_scalar,
@@ -86,6 +87,7 @@
     gram_whole,
     total_ref,
     scalar_sem,
+    token_sem,
     ask_send,
     ask_recv,
     part_send,
@@ -159,6 +161,8 @@
             device_id_type=pl.DeviceIdType.MESH,
         )
 
+    bring = pltpu.make_async_copy(token_home, token_ref, token_sem)
+    bring.start()
     barrier = pltpu.get_barrier_semaphore()
     each_partner(
         lambda there, where: pl.semaphore_signal(
@@ -169,6 +173,7 @@
     each_partner(lambda there, where: ask_copy(there, where, me).start())
 
     total_ref[...] = jnp.zeros_like(total_ref)
+    bring.wait()
     strip = math.gcd(token_ref.shape[0], 2048)
 
     @pl.loop(0, token_ref.shape[0] // strip)
@@ -267,7 +272,7 @@
         halves = split_pair(vectors)
         total_ref[...] = jnp.zeros_like(total_ref)
 
-        @pl.loop(0, inner)
+        @pl.loop(0, inner, unroll=4)
         def _(index):
             rows, product, own, weight = inner_products(index, halves)
             add_rows(jnp.where(own, weight * product, 0.0), rows)
@@ -282,7 +287,7 @@
             value = jnp.where(own, weight * product * product, 0.0)
             return total + jnp.sum(value, axis=1, keepdims=True)
 
-        return lax.fori_loop(0, inner, add, jnp.zeros((host_count, 1), jnp.float32))
+        return lax.fori_loop(0, inner, add, jnp.zeros((host_count, 1), jnp.float32), unroll=4)
 
     def smooth(vectors):
         gram = gram_whole[...].reshape(width, width)
@@ -344,9 +349,10 @@
     return pl.pallas_call(
         functools.partial(solve_body, (outer, inner, capacity)),
         out_shape=jax.ShapeDtypeStruct((host_count, width), jnp.float32),
-        in_specs=[in_vmem] * 4,
+        in_specs=[pl.BlockSpec(memory_space=pl.ANY)] + [in_vmem] * 3,
         out_specs=in_vmem,
         scratch_shapes=[
+            pltpu.VMEM((token_rows, width), jnp.bfloat16),
             pltpu.VMEM((token_rows, width), jnp.float32),
             pltpu.VMEM((device_count, 1, capacity), jnp.int32),
             pltpu.SMEM((device_count, 1, capacity), jnp.int32),
@@ -358,6 +364,7 @@
             pltpu.VMEM((owners, share, width), jnp.float32),
             pltpu.VMEM((host_count, width), jnp.float32),
             pltpu.SemaphoreType.DMA,
+            pltpu.SemaphoreType.DMA,
         ]
         + links,
         compiler_params=pltpu.CompilerParams(

time: 88.2 us -> 84.7 us (0.960)
  Pallas kernels: 80.6 us -> 77.1 us
    pallas_call x1, Pallas kernels: 80.6 us -> 77.1 us  [shards(): pl.pallas_call(functools.partial(solve_body, (outer, inner, capacity)), o...]
where the time goes in v5:
time: 84.7 us; the launch traced here: 84.3 us
  Pallas kernels  77.1 us (91%)
  local copies, waits for them, and re-layouts  3.69 us (4%)
  other arithmetic  2.04 us (2%)
  matrix products  1.34 us (2%)
    pallas_call x1, Pallas kernels, shards(): pl.pallas_call(functools.partial(solve_body, (outer, inner, capacity)), o...  77.1 us
    unnamed x6, local copies, waits for them, and re-layouts  2.9 us

profile of v5, /device:TPU:0, one launch (start us, length us, event | category | flops | bytes accessed | tf_op | source)
XLA Modules:
  0.0 84.3 jit_solution(18409325722634580172)
XLA Ops:
  0.0 0.0 copy-start.1
  0.0 0.8 broadcast_add_fusion
  0.8 0.7 add_select_fusion.1
  1.5 0.1 copy.7
  1.6 0.1 reshape.321
  1.7 0.1 fusion.15
  1.8 0.1 copy.8
  1.9 0.1 reshape.322
  2.0 0.1 fusion.16
  2.1 0.1 fusion.12
  2.2 0.1 pad_maximum_fusion
  2.3 0.1 copy.9
  2.4 0.1 eq.47
  2.5 0.1 eq.43
  2.6 0.1 convert_reduce_fusion
  2.7 0.1 fusion.18
  2.9 0.3 fusion.4
  3.3 0.1 broadcast_multiply_fusion
  3.3 0.9 %fusion.5 = s32[64,256]{1,0:T(8,128)S(1)} fusion(bf16[4096,64]{0,1:T(8,128)(2,1)S(1)} %bitcast.18, s32[4096]{0:T(1024)S(1)} %bitcast.20), kind=kOutput, calls=%fused_computation.7 | convolution fusion | flops 135282688 | bytes 606208 | tf_op jit(solution)/shard_map/dot_general | solution.py:58
  4.3 0.0 copy-done.1
  4.3 0.0 copy-start
  4.3 2.2 %copy-done = bf16[8192,256]{1,0:T(8,128)(2,1)S(1)} copy-done((bf16[8192,256]{1,0:T(8,128)(2,1)S(1)}, bf16[8192,256]{1,0:T(8,128)(2,1)}, u32[]{:S(2)}) %copy-start) | copy-done | bytes 4194328
  6.5 77.1 %shard_map.55 = f32[256,256]{1,0:T(8,128)S(1)} custom-call(bf16[8192,256]{1,0:T(8,128)(2,1)S(1)} %copy-done, s32[16,1,256]{2,1,0:T(1,128)S(1)} %add.110.wanted_ref, s32[4,1,1024]{2,1,0:T(1,128)S(1)} %reshape.323.code_ref, f32[256,256]{1,0:T(8,128)S(1)} %copy-done.1), custom_call_target="tpu_custom_call" | custom-call | tf_op jit(solution)/shard_map/pallas_call | solution.py:349
  83.6 0.7 copy.16
  (9 shorter events, 0.1 us)
Async XLA Ops:
  0.0 4.3 %copy-start.1 = (f32[256,256]{1,0:T(8,128)S(1)}, f32[256,256]{1,0:T(8,128)}, u32[]{:S(2)}) copy-start(f32[256,256]{1,0:T(8,128)} %start_ref.1) | copy-start | bytes 786436
  4.3 2.2 %copy-start = (bf16[8192,256]{1,0:T(8,128)(2,1)S(1)}, bf16[8192,256]{1,0:T(8,128)(2,1)}, u32[]{:S(2)}) copy-start(bf16[8192,256]{1,0:T(8,128)(2,1)} %token_home.1) | copy-start | bytes 12582916

commit v6 on v5

--- a/solution.py
+++ b/solution.py
@@ -270,14 +270,14 @@
 
     def spread(vectors):
         halves = split_pair(vectors)
-        total_ref[...] = jnp.zeros_like(total_ref)
-
-        @pl.loop(0, inner, unroll=4)
-        def _(index):
+
+        def add(index, total):
             rows, product, own, weight = inner_products(index, halves)
-            add_rows(jnp.where(own, weight * product, 0.0), rows)
-
-        return total_ref[...]
+            masked = split_pair(jnp.where(own, weight * product, 0.0))
+            out = jnp.dot(masked, rows, preferred_element_type=jnp.float32)
+            return total + (out[:host_count] + out[host_count:])
+
+        return lax.fori_loop(0, inner, add, jnp.zeros((host_count, width), jnp.float32), unroll=4)
 
     def squares(vectors):
         halves = split_pair(vectors)

time: 84.7 us -> 84.7 us (level)
  no operation moved by 1% of the time
where the time goes in v6:
time: 84.7 us; the launch traced here: 84.4 us
  Pallas kernels  77.1 us (91%)
  local copies, waits for them, and re-layouts  3.69 us (4%)
  other arithmetic  2.04 us (2%)
  matrix products  1.34 us (2%)
    pallas_call x1, Pallas kernels, shards(): pl.pallas_call(functools.partial(solve_body, (outer, inner, capacity)), o...  77.1 us
    unnamed x6, local copies, waits for them, and re-layouts  2.9 us

profile of v6, /device:TPU:0, one launch (start us, length us, event | category | flops | bytes accessed | tf_op | source)
XLA Modules:
  0.0 84.4 jit_solution(12242328017506163925)
XLA Ops:
  0.0 0.0 copy-start.1
  0.0 0.8 broadcast_add_fusion
  0.8 0.7 add_select_fusion.1
  1.5 0.1 copy.7
  1.6 0.1 reshape.321
  1.7 0.1 fusion.15
  1.8 0.1 copy.8
  1.9 0.1 reshape.322
  2.0 0.1 fusion.16
  2.1 0.1 fusion.12
  2.2 0.1 pad_maximum_fusion
  2.3 0.1 copy.9
  2.4 0.1 eq.47
  2.5 0.1 eq.43
  2.6 0.1 convert_reduce_fusion
  2.7 0.1 fusion.18
  2.9 0.3 fusion.4
  3.3 0.1 broadcast_multiply_fusion
  3.3 0.9 %fusion.5 = s32[64,256]{1,0:T(8,128)S(1)} fusion(bf16[4096,64]{0,1:T(8,128)(2,1)S(1)} %bitcast.18, s32[4096]{0:T(1024)S(1)} %bitcast.20), kind=kOutput, calls=%fused_computation.7 | convolution fusion | flops 135282688 | bytes 606208 | tf_op jit(solution)/shard_map/dot_general | solution.py:58
  4.3 0.0 copy-done.1
  4.3 0.0 copy-start
  4.3 2.2 %copy-done = bf16[8192,256]{1,0:T(8,128)(2,1)S(1)} copy-done((bf16[8192,256]{1,0:T(8,128)(2,1)S(1)}, bf16[8192,256]{1,0:T(8,128)(2,1)}, u32[]{:S(2)}) %copy-start) | copy-done | bytes 4194328
  6.5 77.1 %shard_map.55 = f32[256,256]{1,0:T(8,128)S(1)} custom-call(bf16[8192,256]{1,0:T(8,128)(2,1)S(1)} %copy-done, s32[16,1,256]{2,1,0:T(1,128)S(1)} %add.110.wanted_ref, s32[4,1,1024]{2,1,0:T(1,128)S(1)} %reshape.323.code_ref, f32[256,256]{1,0:T(8,128)S(1)} %copy-done.1), custom_call_target="tpu_custom_call" | custom-call | tf_op jit(solution)/shard_map/pallas_call | solution.py:349
  83.7 0.7 copy.16
  (9 shorter events, 0.1 us)
Async XLA Ops:
  0.0 4.3 %copy-start.1 = (f32[256,256]{1,0:T(8,128)S(1)}, f32[256,256]{1,0:T(8,128)}, u32[]{:S(2)}) copy-start(f32[256,256]{1,0:T(8,128)} %start_ref.1) | copy-start | bytes 786436
  4.3 2.2 %copy-start = (bf16[8192,256]{1,0:T(8,128)(2,1)S(1)}, bf16[8192,256]{1,0:T(8,128)(2,1)}, u32[]{:S(2)}) copy-start(bf16[8192,256]{1,0:T(8,128)(2,1)} %token_home.1) | copy-start | bytes 12582916
